TPU v7x, 32 devices: a whole 2x2x4 slice. The times are simulated.
32 devices in a mesh: tile: 8 (over y, x, core), view: 4 (over z).
Axes of the slice: x: 2, y: 2, z: 4, core: 2. Of those that a mesh axis runs over, the one named last changes fastest.
Arguments:
- initial: float32 [8, 4, 256, 256], P('tile'), may hold values from 0.5 to 2
- recorded: float32 [4, 8, 4, 256, 256], P('view', 'tile'), may hold values from 0.2 to 3
- tap_table: float32 [4, 8, 3, 31], P('view'), may hold values from 0.02 to 1
- variants: int32 [4, 8], P('view'), may hold values from 0 to 7
Outputs:
- estimate: float32 [8, 4, 256, 256], P('tile')
Inputs may be any that keep to these rules, and one draw needn't show every extreme that they name: `variants`: indices of the 8 tap tables of the view.
All inputs are finite; a program needn't handle non-finite values.
Results may differ from a plain program's by a relative error of at most 0.0001.
Values sent between devices are 32-bit elements; how exact they have to be, the bound alone decides.
A program may use at most 192 MiB of HBM per device.

v0:
```python
import jax
import jax.numpy as jnp
from jax import lax
from jax.experimental import pallas as pl
from jax.experimental.pallas import tpu as pltpu
from jax.sharding import PartitionSpec as P

GX = 8
ITERS = 2
HALF = 15
EDGE = 16
MESH = pl.DeviceIdType.MESH


def passed_along(block, axis, distance):
    devices = range(lax.axis_size(axis))
    route = [(i - distance, i) for i in devices if i - distance in devices]
    return lax.ppermute(block, axis, route)


def normalized(tap_table):
    return tap_table / jnp.sum(tap_table, axis=-1, keepdims=True)


def tile_kernels(kernels, variant_ids, grid_rows, grid_cols):
    count_variants = kernels.shape[0]
    onehot = (variant_ids[:, None] == jnp.arange(count_variants, dtype=jnp.int32)[None, :]).astype(
        jnp.float32
    )
    flat = jnp.dot(onehot, kernels.reshape(count_variants, -1), precision=lax.Precision.HIGHEST)
    return flat.reshape(grid_rows, grid_cols, 3, kernels.shape[-1])


def tile_onehot(positions, extent, count):
    owner = jnp.clip(jnp.floor_divide(positions, extent), 0, count - 1)
    return (owner[:, None] == jnp.arange(count, dtype=jnp.int32)[None, :]).astype(jnp.float32)


def weight_map(tile_taps, axis_id, offset, row_hot, col_hot):
    inner = jnp.dot(row_hot, tile_taps[:, :, axis_id, offset], precision=lax.Precision.HIGHEST)
    return jnp.dot(inner, col_hot.T, precision=lax.Precision.HIGHEST)


def blur_cols(padded, tile_taps, row_hot, col_hot):
    count = col_hot.shape[0]
    result = jnp.zeros((padded.shape[0], padded.shape[1], count), jnp.float32)
    for offset in range(tile_taps.shape[3]):
        weights = weight_map(tile_taps, 0, offset, row_hot, col_hot)
        result = result + weights[None] * padded[:, :, offset : offset + count]
    return result


def blur_rows(padded, tile_taps, row_hot, col_hot):
    count = row_hot.shape[0]
    result = jnp.zeros((padded.shape[0], count, padded.shape[2]), jnp.float32)
    for offset in range(tile_taps.shape[3]):
        weights = weight_map(tile_taps, 1, offset, row_hot, col_hot)
        result = result + weights[None] * padded[:, offset : offset + count, :]
    return result


def blur_planes(field, tile_taps, row_hot, col_hot, reverse):
    taps = tile_taps.shape[3]
    margin = taps // 2
    padded = jnp.pad(field, ((margin, margin), (0, 0), (0, 0)))
    planes = field.shape[0]
    result = jnp.zeros(field.shape, jnp.float32)
    for offset in range(taps):
        which = taps - 1 - offset if reverse else offset
        weights = weight_map(tile_taps, 2, which, row_hot, col_hot)
        result = result + weights[None] * padded[offset : offset + planes]
    return result


def adjoint_rows(padded, tile_taps, row_hot, col_hot):
    margin = tile_taps.shape[3] // 2
    count = padded.shape[1] - 2 * margin
    result = jnp.zeros((padded.shape[0], count, padded.shape[2]), jnp.float32)
    for offset in range(tile_taps.shape[3]):
        lead = 2 * margin - offset
        weights = weight_map(tile_taps, 1, offset, row_hot, col_hot)
        result = result + weights[None, lead : lead + count, :] * padded[:, lead : lead + count, :]
    return result


def adjoint_cols(padded, tile_taps, row_hot, col_hot):
    margin = tile_taps.shape[3] // 2
    count = padded.shape[2] - 2 * margin
    result = jnp.zeros((padded.shape[0], padded.shape[1], count), jnp.float32)
    for offset in range(tile_taps.shape[3]):
        lead = 2 * margin - offset
        weights = weight_map(tile_taps, 0, offset, row_hot, col_hot)
        result = result + weights[None, :, lead : lead + count] * padded[:, :, lead : lead + count]
    return result


def widen_cols(field, width, tile_col):
    west_send = field[:, :, -width:]
    east_send = field[:, :, :width]
    west_send = jnp.where(tile_col < GX - 1, west_send, jnp.zeros_like(west_send))
    east_send = jnp.where(tile_col > 0, east_send, jnp.zeros_like(east_send))
    from_west = passed_along(west_send, "tile", 1)
    from_east = passed_along(east_send, "tile", -1)
    return jnp.concatenate([from_west, field, from_east], axis=2)


def widen_rows(field, width):
    from_north = passed_along(field[:, -width:, :], "tile", GX)
    from_south = passed_along(field[:, :width, :], "tile", -GX)
    return jnp.concatenate([from_north, field, from_south], axis=1)


def per_device(initial, recorded, tap_table, variants):
    position = lax.axis_index("tile")
    count_tiles = lax.axis_size("tile")
    count_views = lax.axis_size("view")
    grid_rows = count_tiles // GX
    tile_row = position // GX
    tile_col = position % GX
    tile_taps = tile_kernels(normalized(tap_table[0]), variants[0], grid_rows, GX)
    estimate = initial[0]
    observed = recorded[0, 0]
    tall = estimate.shape[1]
    broad = estimate.shape[2]
    row_first = tile_row * tall
    col_first = tile_col * broad

    def row_places(margin):
        return row_first + jnp.arange(tall + 2 * margin, dtype=jnp.int32) - margin

    def col_places(margin):
        return col_first + jnp.arange(broad + 2 * margin, dtype=jnp.int32) - margin

    own_rows = tile_onehot(row_places(0), tall, grid_rows)
    own_cols = tile_onehot(col_places(0), broad, GX)
    wide_rows = tile_onehot(row_places(HALF), tall, grid_rows)
    wide_cols = tile_onehot(col_places(HALF), broad, GX)
    for step in range(ITERS):
        padded = widen_cols(estimate, HALF, tile_col)
        planes = blur_planes(
            blur_cols(padded, tile_taps, own_rows, own_cols), tile_taps, own_rows, own_cols, False
        )
        blurred = blur_rows(widen_rows(planes, HALF), tile_taps, own_rows, own_cols)
        ratio = observed / blurred
        back = adjoint_rows(widen_rows(ratio, HALF), tile_taps, wide_rows, own_cols)
        back = blur_planes(back, tile_taps, own_rows, own_cols, True)
        correction = adjoint_cols(widen_cols(back, HALF, tile_col), tile_taps, own_rows, wide_cols)
        logged = jnp.log(correction)
        summed = lax.psum(logged, "view")
        estimate = estimate * jnp.exp(summed / count_views)
    return estimate[None]


def split(value):
    high = value.astype(jnp.bfloat16)
    return high, (value - high.astype(jnp.float32)).astype(jnp.bfloat16)


def product(left, right, contract):
    dims = (((contract[0],), (contract[1],)), ((), ()))

    def one(a, b):
        return lax.dot_general(a, b, dims, preferred_element_type=jnp.float32)

    return one(left[0], right[0]) + (one(left[0], right[1]) + one(left[1], right[0]))


def strips_kernel(
    init_ref,
    rec_ref,
    tap_ref,
    var_ref,
    out_ref,
    wide_ref,
    flip_ref,
    seen_ref,
    taps_ref,
    g_hi,
    g_lo,
    gt_hi,
    gt_lo,
    m_hi,
    m_lo,
    p_hi,
    p_lo,
    blur_ref,
    corr_ref,
    west_ref,
    east_ref,
    next_ref,
    tap_send,
    tap_recv,
    rec_send,
    rec_recv,
    edge_send,
    edge_recv,
    over_send,
    over_recv,
    halo_send,
    halo_recv,
    out_send,
    out_recv,
):
    tile = lax.axis_index("tile")
    view = lax.axis_index("view")
    tiles = lax.axis_size("tile")
    views = lax.axis_size("view")
    depth, tall, broad = init_ref.shape[1:]
    strip = broad // views
    span = strip + 2 * EDGE
    inner, outer = depth * strip, depth * span
    taps = tap_ref.shape[3]

    def strip_of(position):
        odd = lax.rem(tile, 2)
        return position + odd * (views - 1 - 2 * position)

    mine = strip_of(view)
    has_west = (tile > 0) | (mine > 0)
    has_east = (tile < tiles - 1) | (mine < views - 1)
    step = 1 - 2 * lax.rem(tile, 2)
    west_id = {
        "tile": jnp.where(mine > 0, tile, tile - 1),
        "view": jnp.where(mine > 0, view - step, view),
    }
    east_id = {
        "tile": jnp.where(mine < views - 1, tile, tile + 1),
        "view": jnp.where(mine < views - 1, view + step, view),
    }
    first = pl.multiple_of(mine * strip, strip)

    def peer(shift):
        other = lax.rem(view + shift, views)
        return other, {"tile": tile, "view": other}

    def copy(source, target, send, recv, device):
        return pltpu.make_async_remote_copy(
            src_ref=source,
            dst_ref=target,
            send_sem=send,
            recv_sem=recv,
            device_id=device,
            device_id_type=MESH,
        )

    barrier = pltpu.get_barrier_semaphore()
    for shift in range(1, views):
        pl.semaphore_signal(barrier, inc=1, device_id=peer(shift)[1], device_id_type=MESH)

    @pl.when(tile > 0)
    def _():
        pl.semaphore_signal(
            barrier, inc=1, device_id={"tile": tile - 1, "view": view}, device_id_type=MESH
        )

    @pl.when(tile < tiles - 1)
    def _():
        pl.semaphore_signal(
            barrier, inc=1, device_id={"tile": tile + 1, "view": view}, device_id_type=MESH
        )

    own_taps = tap_ref[0, var_ref[0, tile]]
    own_taps = own_taps / jnp.sum(own_taps, axis=-1, keepdims=True)
    taps_ref[view] = jnp.zeros(taps_ref.shape[1:], jnp.float32)
    taps_ref[view, 0:3, 0:taps] = own_taps
    flip_ref[0] = rec_ref[0, 0, 0].T

    pl.semaphore_wait(
        barrier, views - 1 + jnp.where(tile > 0, 1, 0) + jnp.where(tile < tiles - 1, 1, 0)
    )

    def tap_copy(shift):
        return copy(
            taps_ref.at[view],
            taps_ref.at[view],
            tap_send.at[shift - 1],
            tap_recv.at[view],
            peer(shift)[1],
        )

    for shift in range(1, views):
        tap_copy(shift).start()

    def rec_copy(shift, z):
        other, device = peer(shift)
        rows = pl.ds(pl.multiple_of(strip_of(other) * strip, strip), strip)
        return copy(
            flip_ref.at[z, rows],
            seen_ref.at[view, z],
            rec_send.at[shift - 1, z],
            rec_recv.at[view, z],
            device,
        )

    for z in range(depth):
        if z > 0:
            flip_ref[z] = rec_ref[0, 0, z].T
        for shift in range(1, views):
            rec_copy(shift, z).start()
        seen_ref[view, z] = flip_ref[z, pl.ds(first, strip)]

    for z in range(depth):
        wide_ref[z, EDGE : EDGE + broad] = init_ref[0, z].T

    def edge_west():
        return copy(
            wide_ref.at[:, EDGE : 2 * EDGE],
            wide_ref.at[:, EDGE + broad :],
            edge_send.at[0],
            edge_recv.at[0],
            {"tile": tile - 1, "view": view},
        )

    def edge_east():
        return copy(
            wide_ref.at[:, broad : EDGE + broad],
            wide_ref.at[:, 0:EDGE],
            edge_send.at[1],
            edge_recv.at[1],
            {"tile": tile + 1, "view": view},
        )

    @pl.when(tile > 0)
    def _():
        edge_west().start()

    @pl.when(tile < tiles - 1)
    def _():
        edge_east().start()

    @pl.when(tile == 0)
    def _():
        wide_ref[:, 0:EDGE] = jnp.zeros((depth, EDGE, tall), jnp.float32)

    @pl.when(tile == tiles - 1)
    def _():
        wide_ref[:, EDGE + broad :] = jnp.zeros((depth, EDGE, tall), jnp.float32)

    @pl.when(jnp.logical_not(has_west))
    def _():
        next_ref[:, 0:EDGE] = jnp.zeros((depth, EDGE, tall), jnp.float32)
        west_ref[...] = jnp.zeros(west_ref.shape, jnp.float32)

    @pl.when(jnp.logical_not(has_east))
    def _():
        next_ref[:, EDGE + strip :] = jnp.zeros((depth, EDGE, tall), jnp.float32)
        east_ref[...] = jnp.zeros(east_ref.shape, jnp.float32)

    def places(size, part, axis, shape):
        index = lax.broadcasted_iota(jnp.int32, shape, axis)
        plane = jnp.zeros(shape, jnp.int32)
        for z in range(1, depth):
            plane = plane + jnp.where(index >= z * part, 1, 0)
        return plane, index - plane * part

    def build(v, carry):
        @pl.when(v != view)
        def _():
            copy(
                taps_ref.at[v], taps_ref.at[v], tap_send.at[0], tap_recv.at[v], peer(1)[1]
            ).wait_recv()

        table = taps_ref[v]
        z_out, x_out = places(inner, strip, 0, (inner, outer))
        z_in, x_in = places(outer, span, 1, (inner, outer))
        along_x = x_in - x_out - (EDGE - HALF)
        along_z = z_in - z_out + HALF
        band = jnp.zeros((inner, outer), jnp.float32)
        for c in range(taps):
            band = jnp.where(along_x == c, table[0:1, c : c + 1], band)
        planes = jnp.zeros((inner, outer), jnp.float32)
        for c in range(max(0, HALF - depth + 1), min(taps, HALF + depth)):
            planes = jnp.where(along_z == c, table[2:3, c : c + 1], planes)
        both = band * planes
        g_hi[v], g_lo[v] = split(both)
        gt_hi[v], gt_lo[v] = split(both.T)
        shape = (tall, tall)
        along_y = lax.broadcasted_iota(jnp.int32, shape, 1) - lax.broadcasted_iota(
            jnp.int32, shape, 0
        )
        rows = jnp.zeros(shape, jnp.float32)
        for c in range(taps):
            rows = jnp.where(along_y + HALF == c, table[1:2, c : c + 1], rows)
        m_hi[v], m_lo[v] = split(rows)
        return carry

    lax.fori_loop(0, views, build, 0)

    def over_west(it, v):
        return copy(
            corr_ref.at[it, v, :, 0:EDGE],
            east_ref.at[it, v],
            over_send.at[it, 0, v],
            over_recv.at[it, 0, v],
            west_id,
        )

    def over_east(it, v):
        return copy(
            corr_ref.at[it, v, :, EDGE + strip :],
            west_ref.at[it, v],
            over_send.at[it, 1, v],
            over_recv.at[it, 1, v],
            east_id,
        )

    def halo_west():
        return copy(
            next_ref.at[:, EDGE : 2 * EDGE],
            next_ref.at[:, EDGE + strip :],
            halo_send.at[0],
            halo_recv.at[0],
            west_id,
        )

    def halo_east():
        return copy(
            next_ref.at[:, strip : EDGE + strip],
            next_ref.at[:, 0:EDGE],
            halo_send.at[1],
            halo_recv.at[1],
            east_id,
        )

    def forward(v):
        w = product((g_hi[v], g_lo[v]), (p_hi[...], p_lo[...]), (1, 0))
        return product(split(w), (m_hi[v], m_lo[v]), (1, 1))

    def back(it, v, blurred):
        ratio = seen_ref[v].reshape(inner, tall) / blurred
        a = product(split(ratio), (m_hi[v], m_lo[v]), (1, 0))
        c = product((gt_hi[v], gt_lo[v]), split(a), (1, 0))
        corr_ref[it, v] = c.reshape(depth, span, tall)

        @pl.when(has_west)
        def _():
            over_west(it, v).start()

        @pl.when(has_east)
        def _():
            over_east(it, v).start()

    def summed(it):
        def body(v, total):
            @pl.when(has_east)
            def _():
                over_west(it, v).wait_recv()

            @pl.when(has_west)
            def _():
                over_east(it, v).wait_recv()

            mid = corr_ref[it, v, :, EDGE : EDGE + strip]
            low = mid[:, :EDGE] + west_ref[it, v]
            high = mid[:, strip - EDGE :] + east_ref[it, v]
            full = jnp.concatenate([low, mid[:, EDGE : strip - EDGE], high], axis=1)
            return total + jnp.log(full)

        return lax.fori_loop(0, views, body, jnp.zeros((depth, strip, tall), jnp.float32))

    @pl.when(tile < tiles - 1)
    def _():
        edge_west().wait_recv()

    @pl.when(tile > 0)
    def _():
        edge_east().wait_recv()

    p_hi[...], p_lo[...] = split(wide_ref[:, pl.ds(first, span)].reshape(outer, tall))

    def ahead(v, carry):
        blur_ref[v] = forward(v)
        return carry

    lax.fori_loop(0, views, ahead, 0)

    def first_back(v, carry):
        @pl.when(v != view)
        def _():
            for z in range(depth):
                copy(
                    flip_ref.at[z, pl.ds(0, strip)],
                    seen_ref.at[v, z],
                    rec_send.at[0, z],
                    rec_recv.at[v, z],
                    peer(1)[1],
                ).wait_recv()

        back(0, v, blur_ref[v])
        return carry

    lax.fori_loop(0, views, first_back, 0)
    old = wide_ref[:, pl.ds(pl.multiple_of(first + EDGE, EDGE), strip)]
    new = old * jnp.exp(summed(0) / views)
    next_ref[:, EDGE : EDGE + strip] = new

    @pl.when(has_west)
    def _():
        halo_west().start()

    @pl.when(has_east)
    def _():
        halo_east().start()

    @pl.when(has_east)
    def _():
        halo_west().wait_recv()

    @pl.when(has_west)
    def _():
        halo_east().wait_recv()

    p_hi[...], p_lo[...] = split(next_ref[...].reshape(outer, tall))

    def second(v, carry):
        back(1, v, forward(v))
        return carry

    lax.fori_loop(0, views, second, 0)
    old = next_ref[:, EDGE : EDGE + strip]
    out_ref[0, :, pl.ds(first, strip)] = old * jnp.exp(summed(1) / views)

    def out_copy(shift):
        rows = pl.ds(first, strip)
        return copy(
            out_ref.at[0, :, rows],
            out_ref.at[0, :, rows],
            out_send.at[shift - 1],
            out_recv.at[view],
            peer(shift)[1],
        )

    for shift in range(1, views):
        out_copy(shift).start()
    for shift in range(1, views):
        other = peer(shift)[0]
        rows = pl.ds(pl.multiple_of(strip_of(other) * strip, strip), strip)
        copy(
            out_ref.at[0, :, rows],
            out_ref.at[0, :, rows],
            out_send.at[shift - 1],
            out_recv.at[other],
            peer(shift)[1],
        ).wait_recv()

    for shift in range(1, views):
        tap_copy(shift).wait_send()
        out_copy(shift).wait_send()
        for z in range(depth):
            rec_copy(shift, z).wait_send()

    @pl.when(tile > 0)
    def _():
        edge_west().wait_send()

    @pl.when(tile < tiles - 1)
    def _():
        edge_east().wait_send()

    @pl.when(has_west)
    def _():
        halo_west().wait_send()
        for it in range(ITERS):
            for v in range(views):
                over_west(it, v).wait_send()

    @pl.when(has_east)
    def _():
        halo_east().wait_send()
        for it in range(ITERS):
            for v in range(views):
                over_east(it, v).wait_send()


def by_strips(initial, recorded, tap_table, variants):
    views = lax.axis_size("view")
    depth, tall, broad = initial.shape[1:]
    strip = broad // views
    span = strip + 2 * EDGE
    inner, outer = depth * strip, depth * span
    f32, bf16 = jnp.float32, jnp.bfloat16
    vmem = pl.BlockSpec(memory_space=pltpu.VMEM)
    dma = pltpu.SemaphoreType.DMA
    flipped = pl.pallas_call(
        strips_kernel,
        out_shape=jax.ShapeDtypeStruct((1, depth, broad, tall), f32),
        in_specs=[vmem, vmem, vmem, pl.BlockSpec(memory_space=pltpu.SMEM)],
        out_specs=vmem,
        scratch_shapes=[
            pltpu.VMEM((depth, broad + 2 * EDGE, tall), f32),
            pltpu.VMEM((depth, broad, tall), f32),
            pltpu.VMEM((views, depth, strip, tall), f32),
            pltpu.VMEM((views, 8, 128), f32),
            pltpu.VMEM((views, inner, outer), bf16),
            pltpu.VMEM((views, inner, outer), bf16),
            pltpu.VMEM((views, outer, inner), bf16),
            pltpu.VMEM((views, outer, inner), bf16),
            pltpu.VMEM((views, tall, tall), bf16),
            pltpu.VMEM((views, tall, tall), bf16),
            pltpu.VMEM((outer, tall), bf16),
            pltpu.VMEM((outer, tall), bf16),
            pltpu.VMEM((views, inner, tall), f32),
            pltpu.VMEM((ITERS, views, depth, span, tall), f32),
            pltpu.VMEM((ITERS, views, depth, EDGE, tall), f32),
            pltpu.VMEM((ITERS, views, depth, EDGE, tall), f32),
            pltpu.VMEM((depth, span, tall), f32),
            dma((views - 1,)),
            dma((views,)),
            dma((views - 1, depth)),
            dma((views, depth)),
            dma((2,)),
            dma((2,)),
            dma((ITERS, 2, views)),
            dma((ITERS, 2, views)),
            dma((2,)),
            dma((2,)),
            dma((views - 1,)),
            dma((views,)),
        ],
        compiler_params=pltpu.CompilerParams(
            collective_id=0, has_side_effects=True, vmem_limit_bytes=40 * 2**20
        ),
        name="strips",
    )(initial, recorded, tap_table, variants)
    return jnp.swapaxes(flipped, 2, 3)


def solution(mesh):
    rows_of_tiles = mesh.shape["tile"] // GX
    return jax.shard_map(
        by_strips if rows_of_tiles == 1 else per_device,
        mesh=mesh,
        in_specs=(
            P("tile", None, None, None),
            P("view", "tile", None, None, None),
            P("view", None, None, None),
            P("view", None),
        ),
        out_specs=P("tile", None, None, None),
        check_vma=False,
    )
```

profile of v0, /device:TPU:24, one launch (start us, length us, event | category | flops | bytes accessed | tf_op | source)
XLA Modules:
  0.0 74.2 jit_solution(18168804949276258791)
XLA Ops:
  0.0 0.0 copy-start.2
  0.0 0.7 copy.5.tap_ref
  0.7 0.0 copy-done.2
  0.7 0.0 copy-start
  0.7 1.2 %copy-done = f32[1,4,256,256]{3,2,1,0:T(8,128)S(1)} copy-done((f32[1,4,256,256]{3,2,1,0:T(8,128)S(1)}, f32[1,4,256,256]{3,2,1,0:T(8,128)}, u32[]{:S(2)}) %copy-start) | copy-done | bytes 1048600
  2.0 0.0 copy-start.1
  2.0 1.2 %copy-done.1 = f32[1,1,4,256,256]{4,3,2,1,0:T(8,128)S(1)} copy-done((f32[1,1,4,256,256]{4,3,2,1,0:T(8,128)S(1)}, f32[1,1,4,256,256]{4,3,2,1,0:T(8,128)}, u32[]{:S(2)}) %copy-start.1) | copy-done | bytes 1048600
  3.2 69.7 %strips.1 = f32[1,4,256,256]{3,2,1,0:T(8,128)S(1)} custom-call(f32[1,4,256,256]{3,2,1,0:T(8,128)S(1)} %copy-done, f32[1,1,4,256,256]{4,3,2,1,0:T(8,128)S(1)} %copy-done.1, f32[1,8,3,31]{3,2,1,0:T(4,128)S(1)} %copy.5.tap_ref, s32[1,8]{1,0:T(1,128)S(1)} %copy-done.2), custom_call_target="tpu_custom_call" | custom-call | tf_op jit(solution)/shard_map/strips/pallas_call | solution.py:584
  72.8 1.3 %copy.6 = f32[1,4,256,256]{3,2,1,0:T(8,128)} copy(f32[1,4,256,256]{2,3,1,0:T(8,128)S(1)} %bitcast.1) | data formatting | bytes 2097152 | tf_op jit(solution)/shard_map/transpose | solution.py:625
Async XLA Ops:
  0.0 0.7 copy-start.2
  0.7 1.2 %copy-start = (f32[1,4,256,256]{3,2,1,0:T(8,128)S(1)}, f32[1,4,256,256]{3,2,1,0:T(8,128)}, u32[]{:S(2)}) copy-start(f32[1,4,256,256]{3,2,1,0:T(8,128)} %init_ref.1) | copy-start | bytes 3145732
  2.0 1.2 %copy-start.1 = (f32[1,1,4,256,256]{4,3,2,1,0:T(8,128)S(1)}, f32[1,1,4,256,256]{4,3,2,1,0:T(8,128)}, u32[]{:S(2)}) copy-start(f32[1,1,4,256,256]{4,3,2,1,0:T(8,128)} %rec_ref.1) | copy-start | bytes 3145732
where the time goes:
time: 74.4 us; the launch traced here: 74.2 us
  Pallas kernels  69.7 us (94%)
  local copies, waits for them, and re-layouts  4.48 us (6%)
    pallas_call x1, Pallas kernels, by_strips(): pl.pallas_call(strips_kernel, out_shape=jax.ShapeDtypeStruct((1, depth, b...  69.7 us
    unnamed x7, local copies, waits for them, and re-layouts  3.17 us

commit v1 on v0

--- a/solution.py
+++ b/solution.py
@@ -166,11 +166,14 @@
 
 
 def strips_kernel(
+    init_hbm,
+    rec_hbm,
+    tap_hbm,
+    var_ref,
+    out_ref,
     init_ref,
     rec_ref,
     tap_ref,
-    var_ref,
-    out_ref,
     wide_ref,
     flip_ref,
     seen_ref,
@@ -183,11 +186,14 @@
     m_lo,
     p_hi,
     p_lo,
+    a_hi,
+    a_lo,
     blur_ref,
     corr_ref,
     west_ref,
     east_ref,
     next_ref,
+    load_sem,
     tap_send,
     tap_recv,
     rec_send,
@@ -205,11 +211,23 @@
     view = lax.axis_index("view")
     tiles = lax.axis_size("tile")
     views = lax.axis_size("view")
-    depth, tall, broad = init_ref.shape[1:]
+    depth, tall, broad = init_ref.shape
     strip = broad // views
     span = strip + 2 * EDGE
     inner, outer = depth * strip, depth * span
-    taps = tap_ref.shape[3]
+    taps = tap_ref.shape[2]
+    parts = (1, 2)
+
+    tap_load = pltpu.make_async_copy(tap_hbm.at[0], tap_ref, load_sem.at[0])
+    init_load = pltpu.make_async_copy(init_hbm.at[0], init_ref, load_sem.at[1])
+    rec_loads = [
+        pltpu.make_async_copy(rec_hbm.at[0, 0, z], rec_ref.at[z], load_sem.at[2 + z])
+        for z in range(depth)
+    ]
+    tap_load.start()
+    for z in range(depth):
+        rec_loads[z].start()
+    init_load.start()
 
     def strip_of(position):
         odd = lax.rem(tile, 2)
@@ -229,8 +247,14 @@
     }
     first = pl.multiple_of(mine * strip, strip)
 
-    def peer(shift):
-        other = lax.rem(view + shift, views)
+    half = views // 2
+    side, place = view // half, lax.rem(view, half)
+
+    def peer(order):
+        if order < half:
+            other = (1 - side) * half + lax.rem(place + order, half)
+        else:
+            other = side * half + lax.rem(place + order - half + 1, half)
         return other, {"tile": tile, "view": other}
 
     def copy(source, target, send, recv, device):
@@ -244,7 +268,7 @@
         )
 
     barrier = pltpu.get_barrier_semaphore()
-    for shift in range(1, views):
+    for shift in range(views - 1):
         pl.semaphore_signal(barrier, inc=1, device_id=peer(shift)[1], device_id_type=MESH)
 
     @pl.when(tile > 0)
@@ -259,11 +283,15 @@
             barrier, inc=1, device_id={"tile": tile + 1, "view": view}, device_id_type=MESH
         )
 
-    own_taps = tap_ref[0, var_ref[0, tile]]
-    own_taps = own_taps / jnp.sum(own_taps, axis=-1, keepdims=True)
+    tap_load.wait()
+    chosen = lax.broadcasted_iota(jnp.int32, tap_ref.shape[1:], 0) == var_ref[0, tile]
     taps_ref[view] = jnp.zeros(taps_ref.shape[1:], jnp.float32)
-    taps_ref[view, 0:3, 0:taps] = own_taps
-    flip_ref[0] = rec_ref[0, 0, 0].T
+    for a in range(tap_ref.shape[0]):
+        own_taps = jnp.sum(jnp.where(chosen, tap_ref[a], 0.0), axis=0, keepdims=True)
+        own_taps = own_taps / jnp.sum(own_taps, axis=-1, keepdims=True)
+        taps_ref[view, a : a + 1, 0:taps] = own_taps
+    rec_loads[0].wait()
+    flip_ref[0] = rec_ref[0].T
 
     pl.semaphore_wait(
         barrier, views - 1 + jnp.where(tile > 0, 1, 0) + jnp.where(tile < tiles - 1, 1, 0)
@@ -273,12 +301,12 @@
         return copy(
             taps_ref.at[view],
             taps_ref.at[view],
-            tap_send.at[shift - 1],
+            tap_send.at[shift],
             tap_recv.at[view],
             peer(shift)[1],
         )
 
-    for shift in range(1, views):
+    for shift in range(views - 1):
         tap_copy(shift).start()
 
     def rec_copy(shift, z):
@@ -287,20 +315,25 @@
         return copy(
             flip_ref.at[z, rows],
             seen_ref.at[view, z],
-            rec_send.at[shift - 1, z],
+            rec_send.at[shift, z],
             rec_recv.at[view, z],
             device,
         )
 
     for z in range(depth):
         if z > 0:
-            flip_ref[z] = rec_ref[0, 0, z].T
-        for shift in range(1, views):
+            rec_loads[z].wait()
+            flip_ref[z] = rec_ref[z].T
+        rec_copy(0, z).start()
+        seen_ref[view, z] = flip_ref[z, pl.ds(first, strip)]
+
+    for shift in range(1, views - 1):
+        for z in range(depth):
             rec_copy(shift, z).start()
-        seen_ref[view, z] = flip_ref[z, pl.ds(first, strip)]
-
+
+    init_load.wait()
     for z in range(depth):
-        wide_ref[z, EDGE : EDGE + broad] = init_ref[0, z].T
+        wide_ref[z, EDGE : EDGE + broad] = init_ref[z].T
 
     def edge_west():
         return copy(
@@ -386,23 +419,34 @@
 
     lax.fori_loop(0, views, build, 0)
 
-    def over_west(it, v):
-        return copy(
-            corr_ref.at[it, v, :, 0:EDGE],
-            east_ref.at[it, v],
-            over_send.at[it, 0, v],
-            over_recv.at[it, 0, v],
+    def over_west(it, v, part):
+        planes = pl.ds(part * (depth // parts[it]), depth // parts[it])
+        return copy(
+            corr_ref.at[it, v, planes, 0:EDGE],
+            east_ref.at[it, v, planes],
+            over_send.at[it, 0, v, part],
+            over_recv.at[it, 0, v, part],
             west_id,
         )
 
-    def over_east(it, v):
-        return copy(
-            corr_ref.at[it, v, :, EDGE + strip :],
-            west_ref.at[it, v],
-            over_send.at[it, 1, v],
-            over_recv.at[it, 1, v],
+    def over_east(it, v, part):
+        planes = pl.ds(part * (depth // parts[it]), depth // parts[it])
+        return copy(
+            corr_ref.at[it, v, planes, EDGE + strip :],
+            west_ref.at[it, v, planes],
+            over_send.at[it, 1, v, part],
+            over_recv.at[it, 1, v, part],
             east_id,
         )
+
+    def send_over(it, v, part):
+        @pl.when(has_west)
+        def _():
+            over_west(it, v, part).start()
+
+        @pl.when(has_east)
+        def _():
+            over_east(it, v, part).start()
 
     def halo_west():
         return copy(
@@ -422,41 +466,40 @@
             east_id,
         )
 
-    def forward(v):
-        w = product((g_hi[v], g_lo[v]), (p_hi[...], p_lo[...]), (1, 0))
-        return product(split(w), (m_hi[v], m_lo[v]), (1, 1))
-
-    def back(it, v, blurred):
+    def forward(*vs):
+        spread = [product((g_hi[v], g_lo[v]), (p_hi[...], p_lo[...]), (1, 0)) for v in vs]
+        return [
+            product(split(w), (m_hi[v], m_lo[v]), (1, 1)) for v, w in zip(vs, spread)
+        ]
+
+    def gathered(v, blurred):
         ratio = seen_ref[v].reshape(inner, tall) / blurred
-        a = product(split(ratio), (m_hi[v], m_lo[v]), (1, 0))
-        c = product((gt_hi[v], gt_lo[v]), split(a), (1, 0))
-        corr_ref[it, v] = c.reshape(depth, span, tall)
-
-        @pl.when(has_west)
-        def _():
-            over_west(it, v).start()
-
-        @pl.when(has_east)
-        def _():
-            over_east(it, v).start()
-
-    def summed(it):
-        def body(v, total):
+        return split(product(split(ratio), (m_hi[v], m_lo[v]), (1, 0)))
+
+    def arrived(it, part):
+        def body(v, carry):
             @pl.when(has_east)
             def _():
-                over_west(it, v).wait_recv()
+                over_west(it, v, part).wait_recv()
 
             @pl.when(has_west)
             def _():
-                over_east(it, v).wait_recv()
-
-            mid = corr_ref[it, v, :, EDGE : EDGE + strip]
-            low = mid[:, :EDGE] + west_ref[it, v]
-            high = mid[:, strip - EDGE :] + east_ref[it, v]
-            full = jnp.concatenate([low, mid[:, EDGE : strip - EDGE], high], axis=1)
-            return total + jnp.log(full)
-
-        return lax.fori_loop(0, views, body, jnp.zeros((depth, strip, tall), jnp.float32))
+                over_east(it, v, part).wait_recv()
+
+            return carry
+
+        lax.fori_loop(0, views, body, 0)
+
+    def factor(it, z):
+        total = jnp.zeros((strip, tall), jnp.float32)
+        for v in range(views):
+            mid = corr_ref[it, v, z, EDGE : EDGE + strip]
+            low = mid[:EDGE] + west_ref[it, v, z]
+            high = mid[strip - EDGE :] + east_ref[it, v, z]
+            total = total + jnp.log(
+                jnp.concatenate([low, mid[EDGE : strip - EDGE], high], axis=0)
+            )
+        return jnp.exp(total / views)
 
     @pl.when(tile < tiles - 1)
     def _():
@@ -468,13 +511,16 @@
 
     p_hi[...], p_lo[...] = split(wide_ref[:, pl.ds(first, span)].reshape(outer, tall))
 
-    def ahead(v, carry):
-        blur_ref[v] = forward(v)
+    def ahead(i, carry):
+        blur_ref[2 * i], blur_ref[2 * i + 1] = forward(2 * i, 2 * i + 1)
         return carry
 
-    lax.fori_loop(0, views, ahead, 0)
-
-    def first_back(v, carry):
+    lax.fori_loop(0, views // 2, ahead, 0)
+
+    def first_back(k, carry):
+        from_side = jnp.where(k < half, side, 1 - side)
+        v = from_side * half + lax.rem(place + k, half)
+
         @pl.when(v != view)
         def _():
             for z in range(depth):
@@ -486,13 +532,16 @@
                     peer(1)[1],
                 ).wait_recv()
 
-        back(0, v, blur_ref[v])
+        a = gathered(v, blur_ref[v])
+        corr_ref[0, v] = product((gt_hi[v], gt_lo[v]), a, (1, 0)).reshape(depth, span, tall)
+        send_over(0, v, 0)
         return carry
 
     lax.fori_loop(0, views, first_back, 0)
-    old = wide_ref[:, pl.ds(pl.multiple_of(first + EDGE, EDGE), strip)]
-    new = old * jnp.exp(summed(0) / views)
-    next_ref[:, EDGE : EDGE + strip] = new
+    arrived(0, 0)
+    for z in range(depth):
+        old = wide_ref[z, pl.ds(pl.multiple_of(first + EDGE, EDGE), strip)]
+        next_ref[z, EDGE : EDGE + strip] = old * factor(0, z)
 
     @pl.when(has_west)
     def _():
@@ -512,42 +561,91 @@
 
     p_hi[...], p_lo[...] = split(next_ref[...].reshape(outer, tall))
 
-    def second(v, carry):
-        back(1, v, forward(v))
+    planes = depth // parts[1]
+
+    def spread_back(part, *vs):
+        rows = slice(part * planes * span, (part + 1) * planes * span)
+        for v in vs:
+            c = product((gt_hi[v, rows], gt_lo[v, rows]), (a_hi[v], a_lo[v]), (1, 0))
+            corr_ref[1, v, part * planes : (part + 1) * planes] = c.reshape(planes, span, tall)
+        for v in vs:
+            send_over(1, v, part)
+
+    def second(i, carry):
+        vs = 2 * i, 2 * i + 1
+        for v, blurred in zip(vs, forward(*vs)):
+            a_hi[v], a_lo[v] = gathered(v, blurred)
+        spread_back(0, *vs)
         return carry
 
-    lax.fori_loop(0, views, second, 0)
-    old = next_ref[:, EDGE : EDGE + strip]
-    out_ref[0, :, pl.ds(first, strip)] = old * jnp.exp(summed(1) / views)
-
-    def out_copy(shift):
-        rows = pl.ds(first, strip)
-        return copy(
-            out_ref.at[0, :, rows],
-            out_ref.at[0, :, rows],
-            out_send.at[shift - 1],
-            out_recv.at[view],
-            peer(shift)[1],
-        )
-
-    for shift in range(1, views):
-        out_copy(shift).start()
-    for shift in range(1, views):
-        other = peer(shift)[0]
-        rows = pl.ds(pl.multiple_of(strip_of(other) * strip, strip), strip)
-        copy(
-            out_ref.at[0, :, rows],
-            out_ref.at[0, :, rows],
-            out_send.at[shift - 1],
-            out_recv.at[other],
-            peer(shift)[1],
-        ).wait_recv()
-
-    for shift in range(1, views):
+    lax.fori_loop(0, views // 2, second, 0)
+
+    def rest(i, carry):
+        spread_back(1, 2 * i, 2 * i + 1)
+        return carry
+
+    lax.fori_loop(0, views // 2, rest, 0)
+
+    def out_copy(source, z, way):
+        rows = out_ref.at[
+            0, z, pl.ds(pl.multiple_of(strip_of(source) * strip, strip), strip)
+        ]
+        return copy(
+            rows,
+            rows,
+            out_send.at[way, source, z],
+            out_recv.at[source, z],
+            {"tile": tile, "view": view + 2 * way - 1},
+        )
+
+    for z in range(depth):
+        if z % planes == 0:
+            arrived(1, z // planes)
+        out_ref[0, z, pl.ds(first, strip)] = next_ref[z, EDGE : EDGE + strip] * factor(1, z)
+
+        @pl.when(view < views - 1)
+        def _():
+            out_copy(view, z, 1).start()
+
+        @pl.when(view > 0)
+        def _():
+            out_copy(view, z, 0).start()
+
+    for distance in range(1, views):
+        for z in range(depth):
+
+            @pl.when(view >= distance)
+            def _():
+                out_copy(view - distance, z, 1).wait_recv()
+
+                @pl.when(view < views - 1)
+                def _():
+                    out_copy(view - distance, z, 1).start()
+
+            @pl.when(view + distance < views)
+            def _():
+                out_copy(view + distance, z, 0).wait_recv()
+
+                @pl.when(view > 0)
+                def _():
+                    out_copy(view + distance, z, 0).start()
+
+    for shift in range(views - 1):
         tap_copy(shift).wait_send()
-        out_copy(shift).wait_send()
         for z in range(depth):
             rec_copy(shift, z).wait_send()
+
+    for source in range(views):
+
+        @pl.when((source <= view) & (view < views - 1))
+        def _():
+            for z in range(depth):
+                out_copy(source, z, 1).wait_send()
+
+        @pl.when((source >= view) & (view > 0))
+        def _():
+            for z in range(depth):
+                out_copy(source, z, 0).wait_send()
 
     @pl.when(tile > 0)
     def _():
@@ -562,14 +660,16 @@
         halo_west().wait_send()
         for it in range(ITERS):
             for v in range(views):
-                over_west(it, v).wait_send()
+                for part in range(parts[it]):
+                    over_west(it, v, part).wait_send()
 
     @pl.when(has_east)
     def _():
         halo_east().wait_send()
         for it in range(ITERS):
             for v in range(views):
-                over_east(it, v).wait_send()
+                for part in range(parts[it]):
+                    over_east(it, v, part).wait_send()
 
 
 def by_strips(initial, recorded, tap_table, variants):
@@ -580,13 +680,18 @@
     inner, outer = depth * strip, depth * span
     f32, bf16 = jnp.float32, jnp.bfloat16
     vmem = pl.BlockSpec(memory_space=pltpu.VMEM)
+    anywhere = pl.BlockSpec(memory_space=pl.ANY)
     dma = pltpu.SemaphoreType.DMA
+    by_axis = jnp.swapaxes(tap_table, 1, 2)
     flipped = pl.pallas_call(
         strips_kernel,
         out_shape=jax.ShapeDtypeStruct((1, depth, broad, tall), f32),
-        in_specs=[vmem, vmem, vmem, pl.BlockSpec(memory_space=pltpu.SMEM)],
+        in_specs=[anywhere, anywhere, anywhere, pl.BlockSpec(memory_space=pltpu.SMEM)],
         out_specs=vmem,
         scratch_shapes=[
+            pltpu.VMEM((depth, tall, broad), f32),
+            pltpu.VMEM((depth, tall, broad), f32),
+            pltpu.VMEM(by_axis.shape[1:], f32),
             pltpu.VMEM((depth, broad + 2 * EDGE, tall), f32),
             pltpu.VMEM((depth, broad, tall), f32),
             pltpu.VMEM((views, depth, strip, tall), f32),
@@ -599,29 +704,32 @@
             pltpu.VMEM((views, tall, tall), bf16),
             pltpu.VMEM((outer, tall), bf16),
             pltpu.VMEM((outer, tall), bf16),
+            pltpu.VMEM((views, inner, tall), bf16),
+            pltpu.VMEM((views, inner, tall), bf16),
             pltpu.VMEM((views, inner, tall), f32),
             pltpu.VMEM((ITERS, views, depth, span, tall), f32),
             pltpu.VMEM((ITERS, views, depth, EDGE, tall), f32),
             pltpu.VMEM((ITERS, views, depth, EDGE, tall), f32),
             pltpu.VMEM((depth, span, tall), f32),
+            dma((2 + depth,)),
             dma((views - 1,)),
             dma((views,)),
             dma((views - 1, depth)),
             dma((views, depth)),
             dma((2,)),
             dma((2,)),
-            dma((ITERS, 2, views)),
-            dma((ITERS, 2, views)),
+            dma((ITERS, 2, views, 2)),
+            dma((ITERS, 2, views, 2)),
             dma((2,)),
             dma((2,)),
-            dma((views - 1,)),
-            dma((views,)),
+            dma((2, views, depth)),
+            dma((views, depth)),
         ],
         compiler_params=pltpu.CompilerParams(
-            collective_id=0, has_side_effects=True, vmem_limit_bytes=40 * 2**20
+            collective_id=0, has_side_effects=True, vmem_limit_bytes=56 * 2**20
         ),
         name="strips",
-    )(initial, recorded, tap_table, variants)
+    )(initial, recorded, by_axis, variants)
     return jnp.swapaxes(flipped, 2, 3)
 
 

time: 74.4 us -> 69.1 us (0.929)
  the two profiles are of different devices: /device:TPU:24 before, /device:TPU:0 now
where the time goes in v1:
time: 69.1 us; the launch traced here: 68.8 us
  Pallas kernels  66.3 us (96%)
  local copies, waits for them, and re-layouts  2.53 us (4%)
    pallas_call x1, Pallas kernels, by_strips(): pl.pallas_call(strips_kernel, out_shape=jax.ShapeDtypeStruct((1, depth, b...  66.3 us
    transpose x1, local copies, waits for them, and re-layouts, by_strips(): return jnp.swapaxes(flipped, 2, 3)  2.53 us

profile of v1, /device:TPU:0, one launch (start us, length us, event | category | flops | bytes accessed | tf_op | source)
XLA Modules:
  0.0 68.8 jit_solution(13005834244726977369)
XLA Ops:
  0.0 66.3 %strips.1 = f32[1,4,256,256]{3,2,1,0:T(8,128)} custom-call(f32[1,4,256,256]{3,2,1,0:T(8,128)} %init_hbm.1, f32[1,1,4,256,256]{4,3,2,1,0:T(8,128)} %rec_hbm.1, f32[1,3,8,31]{3,2,1,0:T(8,128)} %bitcast.3, s32[1,8]{1,0:T(1,128)} %var_ref.1), custom_call_target="tpu_custom_call" | custom-call | tf_op jit(solution)/shard_map/strips/pallas_call | solution.py:686
  66.3 2.5 %copy.5 = f32[1,4,256,256]{3,2,1,0:T(8,128)} copy(f32[1,4,256,256]{2,3,1,0:T(8,128)} %bitcast.2) | data formatting | bytes 2097152 | tf_op jit(solution)/shard_map/transpose | solution.py:733

commit v2 on v1

--- a/solution.py
+++ b/solution.py
@@ -186,6 +186,7 @@
     m_lo,
     p_hi,
     p_lo,
+    whole_ref,
     a_hi,
     a_lo,
     blur_ref,
@@ -379,8 +380,8 @@
         next_ref[:, EDGE + strip :] = jnp.zeros((depth, EDGE, tall), jnp.float32)
         east_ref[...] = jnp.zeros(east_ref.shape, jnp.float32)
 
-    def places(size, part, axis, shape):
-        index = lax.broadcasted_iota(jnp.int32, shape, axis)
+    def places(size, part, shape):
+        index = lax.broadcasted_iota(jnp.int32, shape, 1)
         plane = jnp.zeros(shape, jnp.int32)
         for z in range(1, depth):
             plane = plane + jnp.where(index >= z * part, 1, 0)
@@ -394,27 +395,33 @@
             ).wait_recv()
 
         table = taps_ref[v]
-        z_out, x_out = places(inner, strip, 0, (inner, outer))
-        z_in, x_in = places(outer, span, 1, (inner, outer))
-        along_x = x_in - x_out - (EDGE - HALF)
-        along_z = z_in - z_out + HALF
-        band = jnp.zeros((inner, outer), jnp.float32)
+        x_in = lax.broadcasted_iota(jnp.int32, (span, inner), 0)
+        along_x = x_in - places(inner, strip, (span, inner))[1] - (EDGE - HALF)
+        band = jnp.zeros((span, inner), jnp.float32)
         for c in range(taps):
             band = jnp.where(along_x == c, table[0:1, c : c + 1], band)
-        planes = jnp.zeros((inner, outer), jnp.float32)
-        for c in range(max(0, HALF - depth + 1), min(taps, HALF + depth)):
-            planes = jnp.where(along_z == c, table[2:3, c : c + 1], planes)
-        both = band * planes
-        g_hi[v], g_lo[v] = split(both)
-        gt_hi[v], gt_lo[v] = split(both.T)
-        shape = (tall, tall)
-        along_y = lax.broadcasted_iota(jnp.int32, shape, 1) - lax.broadcasted_iota(
-            jnp.int32, shape, 0
-        )
-        rows = jnp.zeros(shape, jnp.float32)
-        for c in range(taps):
-            rows = jnp.where(along_y + HALF == c, table[1:2, c : c + 1], rows)
-        m_hi[v], m_lo[v] = split(rows)
+        z_out = places(inner, strip, (1, inner))[0]
+        for z in range(depth):
+            across = jnp.zeros((1, inner), jnp.float32)
+            for c in range(max(0, HALF - depth + 1), min(taps, HALF + depth)):
+                across = jnp.where(z - z_out + HALF == c, table[2:3, c : c + 1], across)
+            block = band * across
+            rows = slice(z * span, (z + 1) * span)
+            gt_hi[v, rows], gt_lo[v, rows] = split(block)
+            whole_ref[rows] = block
+        g_hi[v], g_lo[v] = split(whole_ref[...].T)
+        chunk = 64 if tall % 64 == 0 else tall
+        for y in range(0, tall, chunk):
+            shape = (chunk, tall)
+            along_y = (
+                lax.broadcasted_iota(jnp.int32, shape, 1)
+                - lax.broadcasted_iota(jnp.int32, shape, 0)
+                + (HALF - y)
+            )
+            lines = jnp.zeros(shape, jnp.float32)
+            for c in range(taps):
+                lines = jnp.where(along_y == c, table[1:2, c : c + 1], lines)
+            m_hi[v, y : y + chunk], m_lo[v, y : y + chunk] = split(lines)
         return carry
 
     lax.fori_loop(0, views, build, 0)
@@ -704,6 +711,7 @@
             pltpu.VMEM((views, tall, tall), bf16),
             pltpu.VMEM((outer, tall), bf16),
             pltpu.VMEM((outer, tall), bf16),
+            pltpu.VMEM((outer, inner), f32),
             pltpu.VMEM((views, inner, tall), bf16),
             pltpu.VMEM((views, inner, tall), bf16),
             pltpu.VMEM((views, inner, tall), f32),

time: 69.1 us -> 69.1 us (level)
  no operation moved by 1% of the time
where the time goes in v2:
time: 69.1 us; the launch traced here: 68.8 us
  Pallas kernels  66.3 us (96%)
  local copies, waits for them, and re-layouts  2.53 us (4%)
    pallas_call x1, Pallas kernels, by_strips(): pl.pallas_call(strips_kernel, out_shape=jax.ShapeDtypeStruct((1, depth, b...  66.3 us
    transpose x1, local copies, waits for them, and re-layouts, by_strips(): return jnp.swapaxes(flipped, 2, 3)  2.53 us

profile of v2, /device:TPU:0, one launch (start us, length us, event | category | flops | bytes accessed | tf_op | source)
XLA Modules:
  0.0 68.8 jit_solution(13165230217340116130)
XLA Ops:
  0.0 66.3 %strips.1 = f32[1,4,256,256]{3,2,1,0:T(8,128)} custom-call(f32[1,4,256,256]{3,2,1,0:T(8,128)} %init_hbm.1, f32[1,1,4,256,256]{4,3,2,1,0:T(8,128)} %rec_hbm.1, f32[1,3,8,31]{3,2,1,0:T(8,128)} %bitcast.3, s32[1,8]{1,0:T(1,128)} %var_ref.1), custom_call_target="tpu_custom_call" | custom-call | tf_op jit(solution)/shard_map/strips/pallas_call | solution.py:693
  66.3 2.5 %copy.5 = f32[1,4,256,256]{3,2,1,0:T(8,128)} copy(f32[1,4,256,256]{2,3,1,0:T(8,128)} %bitcast.2) | data formatting | bytes 2097152 | tf_op jit(solution)/shard_map/transpose | solution.py:741

commit v3 on v2

--- a/solution.py
+++ b/solution.py
@@ -734,7 +734,7 @@
             dma((views, depth)),
         ],
         compiler_params=pltpu.CompilerParams(
-            collective_id=0, has_side_effects=True, vmem_limit_bytes=56 * 2**20
+            collective_id=0, has_side_effects=True, vmem_limit_bytes=52 * 2**20
         ),
         name="strips",
     )(initial, recorded, by_axis, variants)

time: 69.1 us -> 68.1 us (0.986)
  Pallas kernels: 66.3 us -> 65.2 us
    unnamed x0 -> x4, local copies, waits for them, and re-layouts: none -> 1.36 us
    transpose x1, local copies, waits for them, and re-layouts: 2.53 us -> 1.31 us  [by_strips(): return jnp.swapaxes(flipped, 2, 3)]
    pallas_call x1, Pallas kernels: 66.3 us -> 65.2 us  [by_strips(): pl.pallas_call(strips_kernel, out_shape=jax.ShapeDtypeStruct((1, depth, b...]
where the time goes in v3:
time: 68.1 us; the launch traced here: 67.9 us
  Pallas kernels  65.2 us (96%)
  local copies, waits for them, and re-layouts  2.67 us (4%)
    pallas_call x1, Pallas kernels, by_strips(): pl.pallas_call(strips_kernel, out_shape=jax.ShapeDtypeStruct((1, depth, b...  65.2 us

profile of v3, /device:TPU:0, one launch (start us, length us, event | category | flops | bytes accessed | tf_op | source)
XLA Modules:
  0.0 67.9 jit_solution(17161916412992507502)
XLA Ops:
  0.0 0.0 copy-start.1
  0.0 0.7 copy-done.1
  0.7 0.0 copy-start
  0.7 0.7 %copy-done = f32[1,8,3,31]{3,1,2,0:T(8,128)S(1)} copy-done((f32[1,8,3,31]{3,1,2,0:T(8,128)S(1)}, f32[1,8,3,31]{3,1,2,0:T(8,128)}, u32[]{:S(2)}) %copy-start) | copy-done | bytes 3000
  1.4 65.2 %strips.1 = f32[1,4,256,256]{3,2,1,0:T(8,128)S(1)} custom-call(f32[1,4,256,256]{3,2,1,0:T(8,128)} %init_hbm.1, f32[1,1,4,256,256]{4,3,2,1,0:T(8,128)} %rec_hbm.1, f32[1,3,8,31]{3,2,1,0:T(8,128)S(1)} %bitcast.3, s32[1,8]{1,0:T(1,128)S(1)} %copy-done.1), custom_call_target="tpu_custom_call" | custom-call | tf_op jit(solution)/shard_map/strips/pallas_call | solution.py:693
  66.6 1.3 %copy.5 = f32[1,4,256,256]{3,2,1,0:T(8,128)} copy(f32[1,4,256,256]{2,3,1,0:T(8,128)S(1)} %bitcast.2) | data formatting | bytes 2097152 | tf_op jit(solution)/shard_map/transpose | solution.py:741
Async XLA Ops:
  0.0 0.7 copy-start.1
  0.7 0.7 %copy-start = (f32[1,8,3,31]{3,1,2,0:T(8,128)S(1)}, f32[1,8,3,31]{3,1,2,0:T(8,128)}, u32[]{:S(2)}) copy-start(f32[1,8,3,31]{3,1,2,0:T(8,128)} %param.6) | copy-start | bytes 8932
